TPU v7x, 32 devices: a whole 2x2x4 slice. The times are simulated.
32 devices in a mesh: dp: 8 (over z, x), tensor: 4 (over y, core).
Axes of the slice: x: 2, y: 2, z: 4, core: 2. Of those that a mesh axis runs over, the one named last changes fastest.
Arguments:
- query_rows: bfloat16 [16384, 8192], P('dp', 'tensor'), may hold values from -16 to 16
- key_rows: bfloat16 [16384, 1024], P('dp'), may hold values from -10 to 10
- value_rows: bfloat16 [16384, 1024], P('dp'), may hold values from -600 to 600
- segment_ids: int32 [16384], P('dp'), may hold values from 0 to 63, never falling along the last dimension, each value on 1 to 512 neighbouring positions
- norm_gain: float32 [8192], replicated, may hold values from 0.1 to 1.9
- draft_weight: bfloat16 [8192, 512], P('tensor', 'dp'), may hold values from -0.0625 to 0.0625
- targets: bfloat16 [16384, 512], P(('dp', 'tensor')), may hold values from -6 to 6
Outputs:
- grad_weight: float32 [8192, 512], P('tensor', 'dp')
Inputs may be any that keep to these rules, and one draw needn't show every extreme that they name: `segment_ids`: document ids never fall along the tokens; a document has at most 512 tokens, and one has exactly 512.
All inputs are finite; a program needn't handle non-finite values.
Results may differ from a plain program's by a relative error of at most 0.0015.
Values may be sent and summed in bfloat16 or wider, within the bound.
A program may use at most 192 MiB of HBM per device.

v0:
```python
import jax
import jax.numpy as jnp
from jax import lax
from jax.sharding import PartitionSpec as P

D = 8192
HEADS = 64
KV_HEADS = 8
HEAD_DIM = 128


def attend_local(query_rows, key_rows, value_rows, segment_ids):
    length = query_rows.shape[0]
    local_heads = query_rows.shape[1] // HEAD_DIM
    group = HEADS // KV_HEADS
    head_count = max(1, local_heads // group)
    repeats = local_heads // head_count
    first = lax.axis_index("tensor") * local_heads // group
    keys_local = lax.dynamic_slice_in_dim(
        key_rows, first * HEAD_DIM, head_count * HEAD_DIM, 1
    ).reshape(length, head_count, HEAD_DIM)
    values_local = lax.dynamic_slice_in_dim(
        value_rows, first * HEAD_DIM, head_count * HEAD_DIM, 1
    ).reshape(length, head_count, HEAD_DIM)
    grouped = query_rows.reshape(length, head_count, repeats, HEAD_DIM)
    width = min(length, 512)
    scale = HEAD_DIM ** (-0.5)
    places = jnp.arange(length, dtype=jnp.int32)

    def one_block(number):
        offset = number * width
        query_block = lax.dynamic_slice_in_dim(grouped, offset, width, 0)
        block_segments = lax.dynamic_slice_in_dim(segment_ids, offset, width, 0)
        block_places = offset + jnp.arange(width, dtype=jnp.int32)
        allowed = (block_segments[:, None] == segment_ids[None, :]) & (
            block_places[:, None] >= places[None, :]
        )
        scores = (
            jnp.einsum(
                "qgrd,kgd->grqk", query_block, keys_local, preferred_element_type=jnp.float32
            )
            * scale
        )
        scores = jnp.where(allowed[None, None], scores, -1e30)
        shifted = jnp.exp(scores - jnp.max(scores, axis=-1, keepdims=True))
        probs = (shifted / jnp.sum(shifted, axis=-1, keepdims=True)).astype(jnp.bfloat16)
        mixed = jnp.einsum(
            "grqk,kgd->qgrd", probs, values_local, preferred_element_type=jnp.float32
        )
        return mixed.astype(jnp.bfloat16).reshape(width, local_heads * HEAD_DIM)

    outputs = lax.map(one_block, jnp.arange(length // width, dtype=jnp.int32))
    return outputs.reshape(length, local_heads * HEAD_DIM)


def loss_derivative(predicted, targets, total_tokens):
    residual = predicted - targets.astype(jnp.float32)
    return (jnp.clip(residual, -1.0, 1.0) / jnp.sqrt(jnp.float32(total_tokens))).astype(
        jnp.bfloat16
    )


def on_device(query_rows, key_rows, value_rows, segment_ids, norm_gain, draft_weight, targets):
    attended = attend_local(query_rows, key_rows, value_rows, segment_ids)
    length = query_rows.shape[0]
    total_tokens = length * lax.axis_size("dp")
    weight_slab = lax.all_gather(draft_weight, "dp", axis=1, tiled=True)
    slab_rows = weight_slab.shape[0]
    features = attended.astype(jnp.float32)
    squares = jnp.sum(features * features, axis=-1)
    summed = lax.psum(squares, "tensor")
    inverse = lax.rsqrt(summed / D + 1e-06)
    gain_part = lax.dynamic_slice_in_dim(
        norm_gain, lax.axis_index("tensor") * slab_rows, slab_rows, 0
    )
    normed = (features * inverse[:, None] * gain_part[None, :]).astype(jnp.bfloat16)
    picked = normed
    predicted = lax.psum_scatter(
        jnp.dot(picked, weight_slab, preferred_element_type=jnp.float32),
        "tensor",
        scatter_dimension=0,
        tiled=True,
    )
    grad_pred = loss_derivative(predicted, targets, total_tokens)
    picked = normed
    grad_slab = lax.dot_general(
        picked,
        lax.all_gather(grad_pred, "tensor", axis=0, tiled=True),
        (((0,), (0,)), ((), ())),
        preferred_element_type=jnp.float32,
    )
    return lax.psum_scatter(grad_slab, "dp", scatter_dimension=1, tiled=True)


def solution(mesh):
    placed = (
        P("dp", "tensor"),
        P("dp", None),
        P("dp", None),
        P("dp"),
        P(),
        P("tensor", "dp"),
        P(("dp", "tensor"), None),
    )
    return jax.shard_map(
        on_device, mesh=mesh, in_specs=placed, out_specs=P("tensor", "dp"), check_vma=False
    )
```

profile of v0, /device:TPU:9, one launch (start us, length us, event | category | flops | bytes accessed | tf_op | source)
XLA Modules:
  0.0 483.6 jit_solution(16944157185117325675)
XLA Ops:
  7.3 1.7 constant_dynamic-slice_fusion
  9.7 1.3 copy.13
  11.7 12.4 %copy.9 = bf16[2048,2048]{0,1:T(8,128)(2,1)} copy(bf16[2048,2048]{1,0:T(8,128)(2,1)} %param.9) | data formatting | bytes 16777216 | tf_op args[0]
  24.0 251.9 %while.11 = (s32[]{:T(128)}, bf16[4,512,2048]{2,1,0:T(8,128)(2,1)}, s32[4]{0:T(128)S(1)}, s32[2048]{0:T(1024)S(1)}, bf16[2048,2,8,128]{0,3,2,1:T(8,128)(2,1)}, /...) while((s32[]{:T(128)}, bf16[4,512,2048]{2,1,0:T(8,128)(2,1)}, ...), condition=%wide.region_3.4_spmd.clone, body=%wide.region_0.3_spmd.clone.sunk | while | flops 8694794240 | bytes 151079600 | solution.py:52
  25.3 1.2 fusion.59
  26.5 31.3 %fusion.60 = (f32[2,8,512]{2,1,0:T(8,128)S(1)}, f32[2,8,512,2048]{3,2,1,0:T(8,128)}) fusion(pred[512,2048]{1,0:T(8,128)(4,1)S(1)} %fusion.59, bf16[2048,2,8,128]{0,3,2,1:T(8,128)(2,1)} %get-tuple-element.162, s32[]{:T(128)S(6)} %select_n.44, bf16[2048,2,128]{2,0,1:T(8,128)(2,1)} %get-tuple-element.163), kind=kOutput, calls=%fused_computation.36.clone.1 | convolution fusion | flops 4362078208 | bytes 71335936 | tf_op jit(solution)/shard_map/while/body/eval_jaxpr/sub | solution.py:45
  57.8 24.8 %fusion.61 = bf16[2,8,512,128]{2,3,1,0:T(8,128)(2,1)} fusion(f32[2,8,512,2048]{3,2,1,0:T(8,128)} %get-tuple-element.134, f32[2,8,512]{2,1,0:T(8,128)S(1)} %get-tuple-element.135, bf16[2048,2,128]{0,2,1:T(8,128)(2,1)S(1)} %get-tuple-element.164), kind=kOutput, calls=%fused_computation.15.clone.1 | convolution fusion | flops 4329570304 | bytes 70287360 | tf_op jit(solution)/shard_map/while/body/eval_jaxpr/grqk,kgd->qgrd/dot_general | solution.py:47
  82.6 2.9 copy.23
  85.5 1.5 constant_dynamic-update-slice_fusion.2
  88.3 1.2 fusion.59
  89.5 31.3 %fusion.60 = (f32[2,8,512]{2,1,0:T(8,128)S(1)}, f32[2,8,512,2048]{3,2,1,0:T(8,128)}) fusion(pred[512,2048]{1,0:T(8,128)(4,1)S(1)} %fusion.59, bf16[2048,2,8,128]{0,3,2,1:T(8,128)(2,1)} %get-tuple-element.162, s32[]{:T(128)S(6)} %select_n.44, bf16[2048,2,128]{2,0,1:T(8,128)(2,1)} %get-tuple-element.163), kind=kOutput, calls=%fused_computation.36.clone.1 | convolution fusion | flops 4362078208 | bytes 71335936 | tf_op jit(solution)/shard_map/while/body/eval_jaxpr/sub | solution.py:45
  120.8 24.8 %fusion.61 = bf16[2,8,512,128]{2,3,1,0:T(8,128)(2,1)} fusion(f32[2,8,512,2048]{3,2,1,0:T(8,128)} %get-tuple-element.134, f32[2,8,512]{2,1,0:T(8,128)S(1)} %get-tuple-element.135, bf16[2048,2,128]{0,2,1:T(8,128)(2,1)S(1)} %get-tuple-element.164), kind=kOutput, calls=%fused_computation.15.clone.1 | convolution fusion | flops 4329570304 | bytes 70287360 | tf_op jit(solution)/shard_map/while/body/eval_jaxpr/grqk,kgd->qgrd/dot_general | solution.py:47
  145.6 2.9 copy.23
  148.5 1.5 constant_dynamic-update-slice_fusion.2
  151.3 1.2 fusion.59
  152.5 31.3 %fusion.60 = (f32[2,8,512]{2,1,0:T(8,128)S(1)}, f32[2,8,512,2048]{3,2,1,0:T(8,128)}) fusion(pred[512,2048]{1,0:T(8,128)(4,1)S(1)} %fusion.59, bf16[2048,2,8,128]{0,3,2,1:T(8,128)(2,1)} %get-tuple-element.162, s32[]{:T(128)S(6)} %select_n.44, bf16[2048,2,128]{2,0,1:T(8,128)(2,1)} %get-tuple-element.163), kind=kOutput, calls=%fused_computation.36.clone.1 | convolution fusion | flops 4362078208 | bytes 71335936 | tf_op jit(solution)/shard_map/while/body/eval_jaxpr/sub | solution.py:45
  183.8 24.8 %fusion.61 = bf16[2,8,512,128]{2,3,1,0:T(8,128)(2,1)} fusion(f32[2,8,512,2048]{3,2,1,0:T(8,128)} %get-tuple-element.134, f32[2,8,512]{2,1,0:T(8,128)S(1)} %get-tuple-element.135, bf16[2048,2,128]{0,2,1:T(8,128)(2,1)S(1)} %get-tuple-element.164), kind=kOutput, calls=%fused_computation.15.clone.1 | convolution fusion | flops 4329570304 | bytes 70287360 | tf_op jit(solution)/shard_map/while/body/eval_jaxpr/grqk,kgd->qgrd/dot_general | solution.py:47
  208.5 2.9 copy.23
  211.5 1.5 constant_dynamic-update-slice_fusion.2
  215.5 31.3 %fusion.60 = (f32[2,8,512]{2,1,0:T(8,128)S(1)}, f32[2,8,512,2048]{3,2,1,0:T(8,128)}) fusion(pred[512,2048]{1,0:T(8,128)(4,1)S(1)} %fusion.59, bf16[2048,2,8,128]{0,3,2,1:T(8,128)(2,1)} %get-tuple-element.162, s32[]{:T(128)S(6)} %select_n.44, bf16[2048,2,128]{2,0,1:T(8,128)(2,1)} %get-tuple-element.163), kind=kOutput, calls=%fused_computation.36.clone.1 | convolution fusion | flops 4362078208 | bytes 71335936 | tf_op jit(solution)/shard_map/while/body/eval_jaxpr/sub | solution.py:45
  246.8 24.8 %fusion.61 = bf16[2,8,512,128]{2,3,1,0:T(8,128)(2,1)} fusion(f32[2,8,512,2048]{3,2,1,0:T(8,128)} %get-tuple-element.134, f32[2,8,512]{2,1,0:T(8,128)S(1)} %get-tuple-element.135, bf16[2048,2,128]{0,2,1:T(8,128)(2,1)S(1)} %get-tuple-element.164), kind=kOutput, calls=%fused_computation.15.clone.1 | convolution fusion | flops 4329570304 | bytes 70287360 | tf_op jit(solution)/shard_map/while/body/eval_jaxpr/grqk,kgd->qgrd/dot_general | solution.py:47
  271.6 2.9 copy.23
  274.5 1.4 constant_dynamic-update-slice_fusion.2
  275.9 5.1 %multiply_reduce_fusion = f32[4,512]{1,0:T(4,128)S(1)} fusion(bf16[4,512,2048]{2,1,0:T(8,128)(2,1)} %get-tuple-element.47), kind=kLoop, calls=%fused_computation.31 | loop fusion | flops 12580864 | bytes 8396800 | tf_op jit(solution)/shard_map/reduce_sum | solution.py:70
  281.7 5.7 %psum.7 = f32[2048]{0:T(1024)S(1)} all-reduce(f32[2048]{0:T(1024)S(1)} %bitcast.63), channel_id=1, replica_groups=mesh['dp'=8,'tensor'=4] {'tensor'}, use_global_device_ids=true, to_apply=%region_5.6 | all-reduce | flops 2048 | bytes 16384 | tf_op jit(solution)/shard_map/psum | solution.py:71
  287.5 8.6 %fusion.34 = bf16[2048,2048]{1,0:T(8,128)(2,1)} fusion(f32[2048]{0:T(1024)S(1)} %dynamic_slice.21, f32[2048]{0:T(1024)S(1)} %add_rsqrt_fusion, bf16[4,512,2048]{2,1,0:T(8,128)(2,1)} %get-tuple-element.47), kind=kLoop, calls=%fused_computation.30 | loop fusion | flops 16777216 | bytes 16793600 | tf_op jit(solution)/shard_map/convert_element_type | solution.py:76
  296.1 10.6 %fusion.44 = f32[2048,512]{1,0:T(8,128)} fusion(bf16[2048,2048]{1,0:T(8,128)(2,1)} %fusion.34, bf16[2048,512]{0,1:T(8,128)(2,1)} %all-gather.3.cloned.1.call-done), kind=kOutput, calls=%fused_computation.37 | convolution fusion | flops 4294967296 | bytes 14680064 | tf_op jit(solution)/shard_map/dot_general | solution.py:79
  306.7 46.1 %reduce-scatter.3.cloned.1.call-done = f32[512,512]{1,0:T(8,128)} async-done(((f32[2048,512]{1,0:T(8,128)}), f32[512,512]{1,0:T(8,128)}) %reduce-scatter.3.cloned.1.call-update) | async-done | bytes 1048592 | tf_op jit(solution)/shard_map/reduce_scatter | solution.py:78
  352.8 2.2 multiply_convert_fusion
  355.3 22.9 %all-gather.5.cloned.1.call-done = bf16[2048,512]{1,0:T(8,128)(2,1)} async-done(((bf16[512,512]{1,0:T(8,128)(2,1)}), bf16[2048,512]{1,0:T(8,128)(2,1)}) %all-gather.5.cloned.1.call-update) | async-done | bytes 2097168 | tf_op jit(solution)/shard_map/all_gather | solution.py:88
  378.2 10.5 %fusion.45 = f32[2048,512]{0,1:T(8,128)} fusion(bf16[2048,2048]{1,0:T(8,128)(2,1)} %fusion.34, bf16[2048,512]{1,0:T(8,128)(2,1)} %all-gather.5.cloned.1.call-done), kind=kOutput, calls=%fused_computation.38 | convolution fusion | flops 4294967296 | bytes 14680064 | tf_op jit(solution)/shard_map/dot_general | solution.py:86
  388.8 88.3 %reduce-scatter.5.cloned.1.call-done = f32[2048,64]{0,1:T(8,128)} async-done(((f32[2048,512]{0,1:T(8,128)}), f32[2048,64]{0,1:T(8,128)}) %reduce-scatter.5.cloned.1.call-update) | async-done | bytes 524304 | tf_op jit(solution)/shard_map/reduce_scatter | solution.py:92
  (33 shorter events, 7.0 us)
Async XLA Ops:
  6.5 289.5 %all-gather.3.cloned.1.call-start = ((), (), s32[]{:S(2)}) async-start(), calls=%async_computation.2 | async-start | bytes 2359296 | tf_op jit(solution)/shard_map/all_gather | solution.py:67
  7.3 345.6 %reduce-scatter.3.cloned.1.call-start = ((), (), s32[]{:S(2)}) async-start(), calls=%async_computation.3 | async-start | bytes 5242880 | tf_op jit(solution)/shard_map/reduce_scatter | solution.py:78
  11.7 12.4 %copy-start.1 = (s32[2048]{0:T(1024)S(1)}, s32[2048]{0:T(1024)}, u32[]{:S(2)}) copy-start(s32[2048]{0:T(1024)} %param.12) | copy-start | bytes 24580
  296.0 56.8 %copy-start = (bf16[512,512]{1,0:T(8,128)(2,1)S(1)}, bf16[512,512]{1,0:T(8,128)(2,1)}, u32[]{:S(2)}) copy-start(bf16[512,512]{1,0:T(8,128)(2,1)} %param.15) | copy-start | bytes 1572868
  306.6 71.6 %all-gather.5.cloned.1.call-start = ((), (), s32[]{:S(2)}) async-start(), calls=%async_computation.4 | async-start | bytes 2621440 | tf_op jit(solution)/shard_map/all_gather | solution.py:88
  355.0 122.0 %reduce-scatter.5.cloned.1.call-start = ((), (), s32[]{:S(2)}) async-start(), calls=%async_computation.5 | async-start | bytes 4718592 | tf_op jit(solution)/shard_map/reduce_scatter | solution.py:92
Sparse Core Ops, SparseCore 0:
  9.5 49.5 all-gather.2
  306.8 46.0 reduce-scatter.2
  355.2 22.9 all-gather.4
  388.9 88.1 reduce-scatter.4
where the time goes:
time: 486 us; the launch traced here: 484 us
  matrix products  245 us (50%)
  waiting for transfers between devices  158 us (33%)
  local copies, waits for them, and re-layouts  37.7 us (8%)
  other arithmetic  20.6 us (4%)
  between operations  13.2 us (3%)
  blocking collectives  5.73 us (1%)
    sub x4, matrix products, one_block(): shifted = jnp.exp(scores - jnp.max(scores, axis=-1, keepdims=True))  125 us
    dot_general x4, matrix products, one_block(): jnp.einsum('grqk,kgd->qgrd', probs, values_local, preferred_element_type=...  99.1 us
    reduce_scatter x1, waiting for transfers between devices, on_device(): return lax.psum_scatter(grad_slab, 'dp', scatter_dimension=1, tiled=True)  88.3 us
    reduce_scatter x1, waiting for transfers between devices, on_device(): lax.psum_scatter(jnp.dot(picked, weight_slab, preferred_element_type=jnp....  46.1 us
    all_gather x1, waiting for transfers between devices, on_device(): lax.all_gather(grad_pred, 'tensor', axis=0, tiled=True)  22.9 us
    dynamic_update_slice x8, local copies, waits for them, and re-layouts, attend_local(): outputs = lax.map(one_block, jnp.arange(length // width, dtype=jnp.int32))  17.6 us
    unnamed x8, local copies, waits for them, and re-layouts  14.3 us
    dot_general x1, matrix products, on_device(): jnp.dot(picked, weight_slab, preferred_element_type=jnp.float32)  10.6 us
  transfers between devices with their start and end apart: 4, of which 3 were waited for; matrix products, arithmetic and copies ran while one was open for 58% of the time, Pallas kernels for 0%

commit v1 on v0

v1 whole, which is shorter than its diff:
```python
import functools

import jax
import jax.numpy as jnp
from jax import lax
from jax.experimental import pallas as pl
from jax.experimental.pallas import tpu as pltpu
from jax.sharding import PartitionSpec as P

D = 8192
HEADS = 64
KV_HEADS = 8
HEAD_DIM = 128
DOC_MAX = 512
BLOCK = 128
MIB = 1 << 20


def attend_kernel(heads, repeats, first_ref, start_ref, q_ref, k_ref, v_ref, segcol_ref, segrow_ref, o_ref, sq_ref):
    number = pl.program_id(0)
    low = start_ref[number]
    factor = HEAD_DIM ** (-0.5) * 1.4426950408889634
    stack = min(repeats, 4)

    def branch(blocks):
        span = blocks * BLOCK
        offset = pl.multiple_of((number - (blocks - 1)) * BLOCK, BLOCK)
        rows = lax.broadcasted_iota(jnp.int32, (BLOCK, span), 0) + (span - BLOCK)
        cols = lax.broadcasted_iota(jnp.int32, (BLOCK, span), 1)
        seg_k = jnp.concatenate(
            [segrow_ref[number - (blocks - 1) + j] for j in range(blocks)], axis=1
        )
        allowed = (segcol_ref[...] == seg_k) & (rows >= cols)
        bias = jnp.where(allowed, 0.0, -1e30).astype(jnp.float32)
        squares = jnp.zeros((BLOCK, HEAD_DIM), jnp.float32)
        for start in range(0, heads, stack):
            g = start // repeats
            keys = k_ref[pl.ds(offset, span), g * HEAD_DIM : (g + 1) * HEAD_DIM]
            values = v_ref[pl.ds(offset, span), g * HEAD_DIM : (g + 1) * HEAD_DIM]
            queries = jnp.concatenate(
                [q_ref[:, (start + r) * HEAD_DIM : (start + r + 1) * HEAD_DIM] for r in range(stack)],
                axis=0,
            )
            scores = lax.dot_general(
                queries, keys, (((1,), (1,)), ((), ())), preferred_element_type=jnp.float32
            ).reshape(stack, BLOCK, span) + bias[None]
            top = jnp.max(scores, axis=-1, keepdims=True)
            shifted = jnp.exp2((scores - top) * factor)
            total = jnp.sum(shifted, axis=-1, keepdims=True)
            probs = (shifted * (1.0 / total)).astype(jnp.bfloat16).reshape(stack * BLOCK, span)
            mixed = jnp.dot(probs, values, preferred_element_type=jnp.float32).astype(jnp.bfloat16)
            for r in range(stack):
                part = mixed[r * BLOCK : (r + 1) * BLOCK]
                o_ref[:, (start + r) * HEAD_DIM : (start + r + 1) * HEAD_DIM] = part
                wide = part.astype(jnp.float32)
                squares = squares + wide * wide
        sq_ref[0] = jnp.sum(squares.T, axis=0, keepdims=True)

    for blocks in range(1, DOC_MAX // BLOCK + 2):
        pl.when(number - low + 1 == blocks)(functools.partial(branch, blocks))


def attend(query_rows, key_rows, value_rows, segment_ids):
    length, width = query_rows.shape
    heads = width // HEAD_DIM
    group = HEADS // KV_HEADS
    head_count = max(1, heads // group)
    repeats = heads // head_count
    blocks = length // BLOCK
    first = (lax.axis_index("tensor") * heads // group) // head_count
    heads_of_block = segment_ids.reshape(blocks, BLOCK)[:, 0]
    starts = jnp.sum((segment_ids[None, :] < heads_of_block[:, None]).astype(jnp.int32), axis=1) // BLOCK
    kv_spec = pl.BlockSpec((length, head_count * HEAD_DIM), lambda i, f, s: (0, f[0]))
    return pl.pallas_call(
        functools.partial(attend_kernel, heads, repeats),
        out_shape=(
            jax.ShapeDtypeStruct((length, width), jnp.bfloat16),
            jax.ShapeDtypeStruct((blocks, 1, BLOCK), jnp.float32),
        ),
        grid_spec=pltpu.PrefetchScalarGridSpec(
            num_scalar_prefetch=2,
            grid=(blocks,),
            in_specs=[
                pl.BlockSpec((BLOCK, width), lambda i, f, s: (i, 0)),
                kv_spec,
                kv_spec,
                pl.BlockSpec((BLOCK, 1), lambda i, f, s: (i, 0)),
                pl.BlockSpec((blocks, 1, BLOCK), lambda i, f, s: (0, 0, 0)),
            ],
            out_specs=[
                pl.BlockSpec((BLOCK, width), lambda i, f, s: (i, 0)),
                pl.BlockSpec((1, 1, BLOCK), lambda i, f, s: (i, 0, 0)),
            ],
        ),
        compiler_params=pltpu.CompilerParams(vmem_limit_bytes=48 * MIB),
        cost_estimate=pl.CostEstimate(
            flops=4 * length * 512 * width, bytes_accessed=6 * length * width, transcendentals=length * 512 * heads
        ),
    )(
        jnp.reshape(first, (1,)).astype(jnp.int32),
        starts.astype(jnp.int32),
        query_rows,
        key_rows,
        value_rows,
        segment_ids.reshape(length, 1),
        segment_ids.reshape(blocks, 1, BLOCK),
    )


def loss_derivative(predicted, targets, total_tokens):
    residual = predicted - targets.astype(jnp.float32)
    return (jnp.clip(residual, -1.0, 1.0) / jnp.sqrt(jnp.float32(total_tokens))).astype(
        jnp.bfloat16
    )


def on_device(query_rows, key_rows, value_rows, segment_ids, norm_gain, draft_weight, targets):
    attended, squares = attend(query_rows, key_rows, value_rows, segment_ids)
    squares = squares.reshape(-1)
    length = query_rows.shape[0]
    total_tokens = length * lax.axis_size("dp")
    weight_slab = lax.all_gather(draft_weight, "dp", axis=1, tiled=True)
    slab_rows = weight_slab.shape[0]
    features = attended.astype(jnp.float32)
    summed = lax.psum(squares, "tensor")
    inverse = lax.rsqrt(summed / D + 1e-06)
    gain_part = lax.dynamic_slice_in_dim(
        norm_gain, lax.axis_index("tensor") * slab_rows, slab_rows, 0
    )
    normed = (features * inverse[:, None] * gain_part[None, :]).astype(jnp.bfloat16)
    predicted = lax.psum_scatter(
        jnp.dot(normed, weight_slab, preferred_element_type=jnp.float32),
        "tensor",
        scatter_dimension=0,
        tiled=True,
    )
    grad_pred = loss_derivative(predicted, targets, total_tokens)
    grad_slab = lax.dot_general(
        normed,
        lax.all_gather(grad_pred, "tensor", axis=0, tiled=True),
        (((0,), (0,)), ((), ())),
        preferred_element_type=jnp.float32,
    )
    return lax.psum_scatter(grad_slab, "dp", scatter_dimension=1, tiled=True)


def solution(mesh):
    placed = (
        P("dp", "tensor"),
        P("dp", None),
        P("dp", None),
        P("dp"),
        P(),
        P("tensor", "dp"),
        P(("dp", "tensor"), None),
    )
    return jax.shard_map(
        on_device, mesh=mesh, in_specs=placed, out_specs=P("tensor", "dp"), check_vma=False
    )
```

time: 486 us -> 247 us (0.51)
  matrix products: 245 us -> 21.4 us
  Pallas kernels: 0 us -> 33.7 us
  local copies, waits for them, and re-layouts: 37.7 us -> 5.45 us
  other arithmetic: 20.6 us -> 3.12 us
    sub x4 -> x0, matrix products: 125 us -> none  [one_block(): shifted = jnp.exp(scores - jnp.max(scores, axis=-1, keepdims=True))]
    dot_general x6 -> x2, matrix products: 120 us -> 21.4 us  [the longest x1 10.8 us: on_device(): lax.dot_general(normed, lax.all_gather(grad_pred, 'tensor', axis=0, tiled...]
    pallas_call x0 -> x1, Pallas kernels: none -> 33.7 us  [attend(): pl.pallas_call(functools.partial(attend_kernel, heads, repeats), out_shap...]
    dynamic_update_slice x8 -> x0, local copies, waits for them, and re-layouts: 17.6 us -> none  [attend_local(): outputs = lax.map(one_block, jnp.arange(length // width, dtype=jnp.int32))]
    unnamed x8 -> x6, local copies, waits for them, and re-layouts: 14.3 us -> 2.88 us
    convert_element_type x1 -> x0, other arithmetic: 8.56 us -> none  [on_device(): (features * inverse[:, None] * gain_part[None, :]).astype(jnp.bfloat16)]
    all_gather x1, waiting for transfers between devices: 0.01 us -> 5.8 us  [on_device(): weight_slab = lax.all_gather(draft_weight, 'dp', axis=1, tiled=True)]
    dynamic_slice x10 -> x0, local copies, waits for them, and re-layouts: 5.03 us -> none  [the longest x4 2.38 us: attend_local(): outputs = lax.map(one_block, jnp.arange(length // width, dtype=jnp.int32))]
  transfers between devices with their start and end apart: 4 -> 4, of which waited for: 3 -> 4; matrix products, arithmetic and copies ran while one was open for 58% -> 1% of each run, Pallas kernels for 0% -> 14%
where the time goes in v1:
time: 247 us; the launch traced here: 245 us
  waiting for transfers between devices  162 us (66%)
  Pallas kernels  33.7 us (14%)
  matrix products  21.4 us (9%)
  between operations  13.2 us (5%)
  blocking collectives  5.9 us (2%)
  local copies, waits for them, and re-layouts  5.45 us (2%)
  other arithmetic  3.12 us (1%)
    reduce_scatter x1, waiting for transfers between devices, on_device(): return lax.psum_scatter(grad_slab, 'dp', scatter_dimension=1, tiled=True)  88.3 us
    reduce_scatter x1, waiting for transfers between devices, on_device(): lax.psum_scatter(jnp.dot(normed, weight_slab, preferred_element_type=jnp....  44.1 us
    pallas_call x1, Pallas kernels, attend(): pl.pallas_call(functools.partial(attend_kernel, heads, repeats), out_shap...  33.7 us
    all_gather x1, waiting for transfers between devices, on_device(): lax.all_gather(grad_pred, 'tensor', axis=0, tiled=True)  23.1 us
    dot_general x1, matrix products, on_device(): lax.dot_general(normed, lax.all_gather(grad_pred, 'tensor', axis=0, tiled...  10.8 us
    dot_general x1, matrix products, on_device(): jnp.dot(normed, weight_slab, preferred_element_type=jnp.float32)  10.6 us
    psum x1, blocking collectives, on_device(): summed = lax.psum(squares, 'tensor')  5.9 us
    all_gather x1, waiting for transfers between devices, on_device(): weight_slab = lax.all_gather(draft_weight, 'dp', axis=1, tiled=True)  5.8 us
  transfers between devices with their start and end apart: 4, of which 4 were waited for; matrix products, arithmetic and copies ran while one was open for 1% of the time, Pallas kernels for 14%

profile of v1, /device:TPU:9, one launch (start us, length us, event | category | flops | bytes accessed | tf_op | source)
XLA Modules:
  0.0 245.0 jit_solution(6352273499321750761)
XLA Ops:
  6.5 0.0 all-gather.3.cloned.1.call-start
  6.5 0.7 all-gather.3.cloned.1.call-update
  7.3 0.0 reduce-scatter.3.cloned.1.call-start
  7.3 1.1 copy.10.segcol_ref
  8.4 0.7 dynamic_slice.3
  9.1 0.8 slice_reduce_fusion
  9.9 0.9 convert_reduce_fusion
  10.8 0.0 copy-start
  10.8 0.7 copy-done
  11.5 0.0 copy-start.1
  11.5 2.2 copy-done.1
  13.7 33.7 %shard_map.73 = (bf16[2048,2048]{1,0:T(8,128)(2,1)}, f32[16,1,128]{2,1,0:T(1,128)S(1)}) custom-call(s32[1]{0:T(128)} %bitcast.first_ref, s32[16]{0:T(128)S(1)} %and_select_fusion.start_ref, bf16[2048,2048]{1,0:T(8,128)(2,1)} %q_ref.1, bf16[2048,1024]{1,0:T(8,128)(2,1)S(1)} %copy-done.1, bf16[2048,1024]{1,0:T(8,128)(2,1)} %v_ref.1, ...), custom_call_target="tpu_custom_call" | custom-call | flops 8589934592 | bytes 25165824 | tf_op jit(solution)/shard_map/pallas_call | solution.py:74
  47.5 5.9 %psum.7 = f32[2048]{0:T(1024)S(1)} all-reduce(f32[2048]{0:T(1024)S(1)} %bitcast.10), channel_id=1, replica_groups=mesh['dp'=8,'tensor'=4] {'tensor'}, use_global_device_ids=true, to_apply=%region_1.2 | all-reduce | flops 2048 | bytes 16384 | tf_op jit(solution)/shard_map/psum | solution.py:125
  53.4 5.8 %all-gather.3.cloned.1.call-done = bf16[2048,512]{0,1:T(8,128)(2,1)} async-done(((bf16[2048,64]{0,1:T(8,128)(2,1)}), bf16[2048,512]{0,1:T(8,128)(2,1)}) %all-gather.3.cloned.1.call-update) | async-done | bytes 2097168 | tf_op jit(solution)/shard_map/all_gather | solution.py:122
  59.2 0.0 copy-start.2
  59.2 10.6 %fusion.1 = f32[2048,512]{1,0:T(8,128)} fusion(bf16[2048,512]{0,1:T(8,128)(2,1)} %all-gather.3.cloned.1.call-done, bf16[2048,2048]{1,0:T(8,128)(2,1)} %get-tuple-element.7, f32[2048]{0:T(1024)S(1)} %dynamic_slice.3, f32[2048]{0:T(1024)S(1)} %add_rsqrt_fusion), kind=kOutput, calls=%fused_computation.2 | convolution fusion | flops 4311744512 | bytes 14696448 | tf_op jit(solution)/shard_map/dot_general | solution.py:132
  69.8 0.0 reduce-scatter.3.cloned.1.call-update
  69.8 0.0 all-gather.5.cloned.1.call-start
  69.8 44.1 %reduce-scatter.3.cloned.1.call-done = f32[512,512]{1,0:T(8,128)} async-done(((f32[2048,512]{1,0:T(8,128)}), f32[512,512]{1,0:T(8,128)}) %reduce-scatter.3.cloned.1.call-update) | async-done | bytes 1048592 | tf_op jit(solution)/shard_map/reduce_scatter | solution.py:131
  113.9 0.0 copy-done.2
  113.9 2.2 multiply_convert_fusion.3
  116.1 0.0 all-gather.5.cloned.1.call-update
  116.2 0.0 reduce-scatter.5.cloned.1.call-start
  116.2 23.1 %all-gather.5.cloned.1.call-done = bf16[2048,512]{1,0:T(8,128)(2,1)} async-done(((bf16[512,512]{1,0:T(8,128)(2,1)}), bf16[2048,512]{1,0:T(8,128)(2,1)}) %all-gather.5.cloned.1.call-update) | async-done | bytes 2097168 | tf_op jit(solution)/shard_map/all_gather | solution.py:140
  139.3 10.8 %fusion = f32[2048,512]{0,1:T(8,128)} fusion(bf16[2048,512]{1,0:T(8,128)(2,1)} %all-gather.5.cloned.1.call-done, bf16[2048,2048]{1,0:T(8,128)(2,1)} %get-tuple-element.7, f32[2048]{0:T(1024)S(1)} %dynamic_slice.3, f32[2048]{0:T(1024)S(1)} %add_rsqrt_fusion), kind=kOutput, calls=%fused_computation.1 | convolution fusion | flops 4311744512 | bytes 14696448 | tf_op jit(solution)/shard_map/dot_general | solution.py:138
  150.1 0.0 reduce-scatter.5.cloned.1.call-update
  150.2 88.3 %reduce-scatter.5.cloned.1.call-done = f32[2048,64]{0,1:T(8,128)} async-done(((f32[2048,512]{0,1:T(8,128)}), f32[2048,64]{0,1:T(8,128)}) %reduce-scatter.5.cloned.1.call-update) | async-done | bytes 524304 | tf_op jit(solution)/shard_map/reduce_scatter | solution.py:144
  (2 shorter events, 0.0 us)
Async XLA Ops:
  6.5 52.7 %all-gather.3.cloned.1.call-start = ((), (), s32[]{:S(2)}) async-start(), calls=%async_computation.2 | async-start | bytes 2359296 | tf_op jit(solution)/shard_map/all_gather | solution.py:122
  7.3 106.7 %reduce-scatter.3.cloned.1.call-start = ((), (), s32[]{:S(2)}) async-start(), calls=%async_computation.3 | async-start | bytes 5242880 | tf_op jit(solution)/shard_map/reduce_scatter | solution.py:131
  10.8 0.7 copy-start
  11.5 2.2 copy-start.1
  59.2 54.8 %copy-start.2 = (bf16[512,512]{1,0:T(8,128)(2,1)S(1)}, bf16[512,512]{1,0:T(8,128)(2,1)}, u32[]{:S(2)}) copy-start(bf16[512,512]{1,0:T(8,128)(2,1)} %param.13) | copy-start | bytes 1572868
  69.8 69.5 %all-gather.5.cloned.1.call-start = ((), (), s32[]{:S(2)}) async-start(), calls=%async_computation.4 | async-start | bytes 2621440 | tf_op jit(solution)/shard_map/all_gather | solution.py:140
  116.2 122.3 %reduce-scatter.5.cloned.1.call-start = ((), (), s32[]{:S(2)}) async-start(), calls=%async_computation.5 | async-start | bytes 4718592 | tf_op jit(solution)/shard_map/reduce_scatter | solution.py:144
Sparse Core Ops, SparseCore 0:
  9.5 49.6 all-gather.2
  69.9 43.9 reduce-scatter.2
  116.3 22.9 all-gather.4
  150.3 88.1 reduce-scatter.4

commit v2 on v1

--- a/solution.py
+++ b/solution.py
@@ -107,41 +107,249 @@
     )
 
 
-def loss_derivative(predicted, targets, total_tokens):
-    residual = predicted - targets.astype(jnp.float32)
-    return (jnp.clip(residual, -1.0, 1.0) / jnp.sqrt(jnp.float32(total_tokens))).astype(
-        jnp.bfloat16
-    )
+def tail_kernel(
+    teams, shards, x_hbm, w_hbm, sq_ref, gain_ref, target_ref, o_ref,
+    x, w, sq_in, inverse, sib_out, sib_in, keep, far_in, slopes, acc, block, gx_out, gx_in, gz_out, gz_in,
+    local_sem, sq_s, sq_r, sib_s, sib_r, far_s, far_r, own_s, pass_s, slope_r, gx_s, gx_r, gz_s, gz_r,
+):
+    me_t, me_d = lax.axis_index("tensor"), lax.axis_index("dp")
+    pairs, lines = teams // 2, shards // 2
+    k, c = me_t // 2, lax.rem(me_t, 2)
+    h, p = me_d // 2, lax.rem(me_d, 2)
+    length, width = x.shape
+    part = length // teams
+    piece = min(part, 256)
+    columns = w.shape[1]
+    own = columns // shards
+    tokens = float(length * shards)
+    chunk = min(width, 512)
+
+    def copy(src, dst, send, recv, t=None, d=None):
+        return pltpu.make_async_remote_copy(
+            src_ref=src,
+            dst_ref=dst,
+            send_sem=send,
+            recv_sem=recv,
+            device_id=(me_d if d is None else d, me_t if t is None else t),
+            device_id_type=pl.DeviceIdType.MESH,
+        )
+
+    load_x = pltpu.make_async_copy(x_hbm, x, local_sem.at[0])
+    load_w = pltpu.make_async_copy(w_hbm, w, local_sem.at[1])
+    load_x.start()
+    load_w.start()
+
+    barrier = pltpu.get_barrier_semaphore()
+    for j in range(1, teams):
+        pl.semaphore_signal(
+            barrier, inc=1, device_id=(me_d, lax.rem(me_t + j, teams)), device_id_type=pl.DeviceIdType.MESH
+        )
+    for j in range(1, shards):
+        pl.semaphore_signal(
+            barrier, inc=1, device_id=(lax.rem(me_d + j, shards), me_t), device_id_type=pl.DeviceIdType.MESH
+        )
+    pl.semaphore_wait(barrier, teams + shards - 2)
+
+    sent = []
+    for j in range(1, teams):
+        one = copy(sq_ref, sq_in.at[j], sq_s.at[j], sq_r.at[j], t=lax.rem(me_t + j, teams))
+        one.start()
+        sent.append(one)
+    total = sq_ref[...]
+    for j in range(1, teams):
+        sent[j - 1].wait_recv()
+        total = total + sq_in[j]
+    inverse[...] = lax.rsqrt(total / D + 1e-06)
+    load_x.wait()
+    load_w.wait()
+
+    def predict(owner, into):
+        base = owner * part
+
+        def norm(i, carry):
+            rows = pl.ds(pl.multiple_of(base + i * BLOCK, BLOCK), BLOCK)
+            row = inverse[pl.ds(owner * (part // BLOCK) + i, 1), :]
+            column = jnp.broadcast_to(row, (BLOCK, BLOCK)).T[:, :1]
+            x[rows, :] = (x[rows, :].astype(jnp.float32) * column * gain_ref[...]).astype(jnp.bfloat16)
+            return carry
+
+        lax.fori_loop(0, part // BLOCK, norm, 0)
+
+        def multiply(i, carry):
+            rows = pl.ds(pl.multiple_of(base + i * piece, BLOCK), piece)
+            into[pl.ds(pl.multiple_of(i * piece, BLOCK), piece), :] = jnp.dot(
+                x[rows, :], w[...], preferred_element_type=jnp.float32
+            )
+            return carry
+
+        lax.fori_loop(0, part // piece, multiply, 0)
+
+    arriving = {}
+    for j in list(range(1, pairs)) + [0]:
+        kk = lax.rem(k + j, pairs)
+        predict(2 * kk + 1 - c, sib_out.at[j])
+        one = copy(sib_out.at[j], sib_in.at[j], sib_s.at[j], sib_r.at[j], t=2 * k + 1 - c)
+        one.start()
+        sent.append(one)
+        predict(2 * kk + c, keep.at[j])
+        one.wait_recv()
+        keep[j] = keep[j] + sib_in[j]
+        if j:
+            far = copy(keep.at[j], far_in.at[j], far_s.at[j], far_r.at[j], t=2 * kk + c)
+            far.start()
+            sent.append(far)
+            arriving[j] = far
+    for j in range(1, pairs):
+        arriving[j].wait_recv()
+
+    for i in range(part // BLOCK):
+        rows = slice(i * BLOCK, (i + 1) * BLOCK)
+        predicted = keep[0, rows, :]
+        for j in range(1, pairs):
+            predicted = predicted + far_in[j, rows, :]
+        residual = predicted - target_ref[rows, :].astype(jnp.float32)
+        slope = jnp.clip(residual, -1.0, 1.0) / jnp.sqrt(jnp.float32(tokens))
+        slopes[me_t, :, rows] = slope.T.astype(jnp.bfloat16)
+
+    for j in range(1, pairs):
+        kk = lax.rem(k + j, pairs)
+        one = copy(slopes.at[me_t], slopes.at[me_t], own_s.at[j], slope_r.at[me_t], t=2 * kk + c)
+        one.start()
+        sent.append(one)
+    one = copy(slopes.at[me_t], slopes.at[me_t], own_s.at[0], slope_r.at[me_t], t=2 * k + 1 - c)
+    one.start()
+    sent.append(one)
+
+    def arrived(slot):
+        copy(slopes.at[slot], slopes.at[slot], own_s.at[0], slope_r.at[slot], t=2 * k + 1 - c).wait_recv()
+
+    def product(owner, rows, cols):
+        tokens_of = pl.ds(pl.multiple_of(owner * part, BLOCK), part)
+        return jnp.dot(slopes[owner, rows, :], x[tokens_of, cols], preferred_element_type=jnp.float32)
+
+    side = 2 * k + 1 - c
+    arrived(side)
+
+    def early(i, carry):
+        cols = pl.ds(pl.multiple_of(i * chunk, BLOCK), chunk)
+        for r in range(2):
+            rows = slice(r * columns // 2, (r + 1) * columns // 2)
+            acc[rows, cols] = product(me_t, rows, cols) + product(side, rows, cols)
+        return carry
+
+    lax.fori_loop(0, width // chunk, early, 0)
+    for j in range(1, pairs):
+        slot = 2 * lax.rem(k + pairs - j, pairs) + c
+        arrived(slot)
+        one = copy(slopes.at[slot], slopes.at[slot], pass_s.at[j], slope_r.at[slot], t=2 * k + 1 - c)
+        one.start()
+        sent.append(one)
+    for j in range(1, pairs):
+        arrived(2 * lax.rem(k + pairs - j, pairs) + 1 - c)
+
+    crossing = {}
+    for j in list(range(1, lines)) + [0]:
+        hh = lax.rem(h + j, lines)
+        rows = pl.ds(pl.multiple_of(hh * 2 * own, 2 * own), 2 * own)
+
+        def late(i, carry):
+            cols = pl.ds(pl.multiple_of(i * chunk, BLOCK), chunk)
+            value = acc[rows, cols]
+            for m in range(1, pairs):
+                base = 2 * lax.rem(k + m, pairs)
+                value = value + product(base, rows, cols) + product(base + 1, rows, cols)
+            block[j, :, cols] = value
+            return carry
+
+        lax.fori_loop(0, width // chunk, late, 0)
+        gx_out[j] = block[j, pl.ds(pl.multiple_of((1 - p) * own, own), own), :].astype(jnp.bfloat16)
+        one = copy(gx_out.at[j], gx_in.at[j], gx_s.at[j], gx_r.at[j], d=2 * h + 1 - p)
+        one.start()
+        sent.append(one)
+        crossing[j] = one
+
+    mine = pl.ds(pl.multiple_of(p * own, own), own)
+    landing = []
+    for j in range(1, lines):
+        hh = lax.rem(h + j, lines)
+        crossing[j].wait_recv()
+        gz_out[j] = block[j, mine, :] + gx_in[j].astype(jnp.float32)
+        one = copy(gz_out.at[j], gz_in.at[j], gz_s.at[j], gz_r.at[j], d=2 * hh + p)
+        one.start()
+        sent.append(one)
+        landing.append(one)
+    crossing[0].wait_recv()
+    o_ref[...] = block[0, mine, :] + gx_in[0].astype(jnp.float32)
+    for j in range(1, lines):
+        landing[j - 1].wait_recv()
+        o_ref[...] += gz_in[j]
+    for one in sent:
+        one.wait_send()
+
+
+def tail(attended, weight_slab, squares, gain_part, targets):
+    teams, shards = lax.axis_size("tensor"), lax.axis_size("dp")
+    length, width = attended.shape
+    columns = weight_slab.shape[1]
+    pairs, lines, part, own = teams // 2, shards // 2, length // teams, columns // shards
+    vmem = pl.BlockSpec(memory_space=pltpu.VMEM)
+    anywhere = pl.BlockSpec(memory_space=pl.ANY)
+    f32, bf16 = jnp.float32, jnp.bfloat16
+    dma = pltpu.SemaphoreType.DMA
+    return pl.pallas_call(
+        functools.partial(tail_kernel, teams, shards),
+        out_shape=jax.ShapeDtypeStruct((own, width), f32),
+        in_specs=[anywhere, anywhere, vmem, vmem, vmem],
+        out_specs=vmem,
+        scratch_shapes=[
+            pltpu.VMEM((length, width), bf16),
+            pltpu.VMEM((width, columns), bf16),
+            pltpu.VMEM((teams,) + squares.shape, f32),
+            pltpu.VMEM(squares.shape, f32),
+            pltpu.VMEM((pairs, part, columns), f32),
+            pltpu.VMEM((pairs, part, columns), f32),
+            pltpu.VMEM((pairs, part, columns), f32),
+            pltpu.VMEM((pairs, part, columns), f32),
+            pltpu.VMEM((teams, columns, part), bf16),
+            pltpu.VMEM((columns, width), f32),
+            pltpu.VMEM((lines, 2 * own, width), f32),
+            pltpu.VMEM((lines, own, width), bf16),
+            pltpu.VMEM((lines, own, width), bf16),
+            pltpu.VMEM((lines, own, width), f32),
+            pltpu.VMEM((lines, own, width), f32),
+            dma((2,)),
+            dma((teams,)),
+            dma((teams,)),
+            dma((pairs,)),
+            dma((pairs,)),
+            dma((pairs,)),
+            dma((pairs,)),
+            dma((pairs,)),
+            dma((pairs,)),
+            dma((teams,)),
+            dma((lines,)),
+            dma((lines,)),
+            dma((lines,)),
+            dma((lines,)),
+        ],
+        compiler_params=pltpu.CompilerParams(
+            collective_id=0, has_side_effects=True, vmem_limit_bytes=52 * MIB
+        ),
+        cost_estimate=pl.CostEstimate(
+            flops=4 * length * width * columns, bytes_accessed=2 * length * width, transcendentals=0
+        ),
+    )(attended, weight_slab, squares, gain_part, targets)
 
 
 def on_device(query_rows, key_rows, value_rows, segment_ids, norm_gain, draft_weight, targets):
-    attended, squares = attend(query_rows, key_rows, value_rows, segment_ids)
-    squares = squares.reshape(-1)
-    length = query_rows.shape[0]
-    total_tokens = length * lax.axis_size("dp")
     weight_slab = lax.all_gather(draft_weight, "dp", axis=1, tiled=True)
     slab_rows = weight_slab.shape[0]
-    features = attended.astype(jnp.float32)
-    summed = lax.psum(squares, "tensor")
-    inverse = lax.rsqrt(summed / D + 1e-06)
     gain_part = lax.dynamic_slice_in_dim(
         norm_gain, lax.axis_index("tensor") * slab_rows, slab_rows, 0
-    )
-    normed = (features * inverse[:, None] * gain_part[None, :]).astype(jnp.bfloat16)
-    predicted = lax.psum_scatter(
-        jnp.dot(normed, weight_slab, preferred_element_type=jnp.float32),
-        "tensor",
-        scatter_dimension=0,
-        tiled=True,
-    )
-    grad_pred = loss_derivative(predicted, targets, total_tokens)
-    grad_slab = lax.dot_general(
-        normed,
-        lax.all_gather(grad_pred, "tensor", axis=0, tiled=True),
-        (((0,), (0,)), ((), ())),
-        preferred_element_type=jnp.float32,
-    )
-    return lax.psum_scatter(grad_slab, "dp", scatter_dimension=1, tiled=True)
+    ).reshape(1, slab_rows)
+    attended, squares = attend(query_rows, key_rows, value_rows, segment_ids)
+    squares = squares.reshape(-1, BLOCK)
+    return tail(attended, weight_slab, squares, gain_part, targets).T
 
 
 def solution(mesh):

time: 247 us -> 178 us (0.72)
  waiting for transfers between devices: 162 us -> 12.7 us
  Pallas kernels: 33.7 us -> 140 us
  matrix products: 21.4 us -> 0 us
  blocking collectives: 5.9 us -> 0 us
  local copies, waits for them, and re-layouts: 5.45 us -> 10.2 us
    reduce_scatter x2 -> x0, waiting for transfers between devices: 132 us -> none  [the longest x1 88.3 us: on_device(): return lax.psum_scatter(grad_slab, 'dp', scatter_dimension=1, tiled=True)]
    pallas_call x0 -> x1, Pallas kernels: none -> 107 us  [tail(): pl.pallas_call(functools.partial(tail_kernel, teams, shards), out_shape=j...]
    all_gather x1 -> x0, waiting for transfers between devices: 23.1 us -> none  [on_device(): lax.all_gather(grad_pred, 'tensor', axis=0, tiled=True)]
    dot_general x2 -> x0, matrix products: 21.4 us -> none  [the longest x1 10.8 us: on_device(): lax.dot_general(normed, lax.all_gather(grad_pred, 'tensor', axis=0, tiled...]
    all_gather x1, waiting for transfers between devices: 5.8 us -> 12 us  [on_device(): weight_slab = lax.all_gather(draft_weight, 'dp', axis=1, tiled=True)]
    psum x1 -> x0, blocking collectives: 5.9 us -> none  [on_device(): summed = lax.psum(squares, 'tensor')]
    all_gather x0 -> x1, local copies, waits for them, and re-layouts: none -> 3.93 us  [on_device(): weight_slab = lax.all_gather(draft_weight, 'dp', axis=1, tiled=True)]
  transfers between devices with their start and end apart: 4 -> 1, of which waited for: 4 -> 1; matrix products, arithmetic and copies ran while one was open for 1% -> 2% of each run, Pallas kernels for 14% -> 19%
where the time goes in v2:
time: 178 us
  Pallas kernels  140 us (79%)
  between operations  13.5 us (8%)
  waiting for transfers between devices  12.7 us (7%)
  local copies, waits for them, and re-layouts  10.2 us (6%)
    pallas_call x1, Pallas kernels, tail(): pl.pallas_call(functools.partial(tail_kernel, teams, shards), out_shape=j...  107 us
    pallas_call x1, Pallas kernels, attend(): pl.pallas_call(functools.partial(attend_kernel, heads, repeats), out_shap...  33.5 us
    all_gather x1, waiting for transfers between devices, on_device(): weight_slab = lax.all_gather(draft_weight, 'dp', axis=1, tiled=True)  12 us
    all_gather x1, local copies, waits for them, and re-layouts, on_device(): weight_slab = lax.all_gather(draft_weight, 'dp', axis=1, tiled=True)  3.93 us
    unnamed x7, local copies, waits for them, and re-layouts  3.68 us
  transfers between devices with their start and end apart: 1, of which 1 were waited for; matrix products, arithmetic and copies ran while one was open for 2% of the time, Pallas kernels for 19%

profile of v2, /device:TPU:9, one launch (start us, length us, event | category | flops | bytes accessed | tf_op | source)
XLA Modules:
  0.0 177.7 jit_solution(828524181881053883)
XLA Ops:
  6.5 0.0 all-gather.2.cloned.1.call-start
  6.5 0.7 all-gather.2.cloned.1.call-update
  7.3 1.1 copy.15.segcol_ref
  8.4 0.7 dynamic_slice.3
  9.1 0.8 slice_reduce_fusion
  9.9 0.9 convert_reduce_fusion
  10.8 0.0 copy-start
  10.8 0.7 copy-done
  11.5 0.0 copy-start.1
  11.5 2.2 %copy-done.1 = bf16[2048,1024]{1,0:T(8,128)(2,1)S(1)} copy-done((bf16[2048,1024]{1,0:T(8,128)(2,1)S(1)}, bf16[2048,1024]{1,0:T(8,128)(2,1)}, u32[]{:S(2)}) %copy-start.1) | copy-done | bytes 4194328
  13.7 33.5 %shard_map.73 = (bf16[2048,2048]{1,0:T(8,128)(2,1)}, f32[16,1,128]{2,1,0:T(1,128)S(1)}) custom-call(s32[1]{0:T(128)} %bitcast.first_ref, s32[16]{0:T(128)S(1)} %and_select_fusion.start_ref, bf16[2048,2048]{1,0:T(8,128)(2,1)} %q_ref.1, bf16[2048,1024]{1,0:T(8,128)(2,1)S(1)} %copy-done.1, bf16[2048,1024]{1,0:T(8,128)(2,1)} %v_ref.1, ...), custom_call_target="tpu_custom_call" | custom-call | flops 8589934592 | bytes 25165824 | tf_op jit(solution)/shard_map/pallas_call | solution.py:74
  47.2 0.0 copy-start.2
  47.2 12.0 %all-gather.2.cloned.1.call-done = bf16[2048,512]{0,1:T(8,128)(2,1)} async-done(((bf16[2048,64]{0,1:T(8,128)(2,1)}), bf16[2048,512]{0,1:T(8,128)(2,1)}) %all-gather.2.cloned.1.call-update) | async-done | bytes 2097168 | tf_op jit(solution)/shard_map/all_gather | solution.py:345
  59.1 3.9 %copy.16.w_hbm = bf16[2048,512]{1,0:T(8,128)(2,1)} copy(bf16[2048,512]{0,1:T(8,128)(2,1)} %all-gather.2.cloned.1.call-done) | data formatting | bytes 4194304 | tf_op jit(solution)/shard_map/all_gather | solution.py:345
  63.0 0.0 copy-done.2
  63.0 107.0 %shard_map.74 = f32[64,2048]{1,0:T(8,128)S(1)} custom-call(bf16[2048,2048]{1,0:T(8,128)(2,1)} %get-tuple-element.7.x_hbm, bf16[2048,512]{1,0:T(8,128)(2,1)} %copy.16.w_hbm, f32[16,128]{1,0:T(8,128)S(1)} %bitcast.12, f32[1,2048]{1,0:T(1,128)S(1)} %bitcast.11, bf16[512,512]{1,0:T(8,128)(2,1)S(1)} %copy-done.2), custom_call_target="tpu_custom_call" | custom-call | flops 8589934592 | bytes 8388608 | tf_op jit(solution)/shard_map/pallas_call | solution.py:299
  170.0 0.8 copy.18
  (1 shorter events, 0.0 us)
Async XLA Ops:
  6.5 52.6 %all-gather.2.cloned.1.call-start = ((), (), s32[]{:S(2)}) async-start(), calls=%async_computation | async-start | bytes 2359296 | tf_op jit(solution)/shard_map/all_gather | solution.py:345
  10.8 0.7 copy-start
  11.5 2.2 %copy-start.1 = (bf16[2048,1024]{1,0:T(8,128)(2,1)S(1)}, bf16[2048,1024]{1,0:T(8,128)(2,1)}, u32[]{:S(2)}) copy-start(bf16[2048,1024]{1,0:T(8,128)(2,1)} %k_ref.1) | copy-start | bytes 12582916
  47.2 15.9 %copy-start.2 = (bf16[512,512]{1,0:T(8,128)(2,1)S(1)}, bf16[512,512]{1,0:T(8,128)(2,1)}, u32[]{:S(2)}) copy-start(bf16[512,512]{1,0:T(8,128)(2,1)} %target_ref.1) | copy-start | bytes 1572868
Sparse Core Ops, SparseCore 0:
  9.5 49.5 all-gather.1
